TPU v7x, 32 devices: a whole 2x2x4 slice. The times are simulated.
32 devices in a mesh: gx: 2 (over x), gy: 4 (over y, core), gz: 4 (over z).
Axes of the slice: x: 2, y: 2, z: 4, core: 2. Of those that a mesh axis runs over, the one named last changes fastest.
Arguments:
- residual: bfloat16 [2, 4, 4, 6, 32, 512], P('gx', 'gy', 'gz'), may hold values from -6 to 6
- panel: bfloat16 [2, 4, 4, 6, 1024, 512], P('gx', 'gy', 'gz'), may hold values from -0.1875 to 0.1875
- face_block: bfloat16 [2, 4, 4, 6, 512, 512], P('gx', 'gy', 'gz'), may hold values from -0.25 to 0.25
- deluxe_inv: bfloat16 [2, 4, 4, 6, 512, 512], P('gx', 'gy', 'gz'), may hold values from -0.25 to 0.25
- basis: bfloat16 [2, 4, 4, 6, 24, 512], P('gx', 'gy', 'gz'), may hold values from -0.25 to 0.25
- face_size: int32 [2, 4, 4, 6], P('gx', 'gy', 'gz'), may hold values from 128 to 512, as said below
- coarse_idx: int32 [2, 4, 4, 6, 24], P('gx', 'gy', 'gz'), may hold values from 0 to 63, as said below
- coarse_scale: float32 [2, 4, 4, 32], P('gx', 'gy', 'gz'), may hold values from 0.5 to 4
Outputs:
- corrected: bfloat16 [2, 4, 4, 6, 32, 512], P('gx', 'gy', 'gz')
Inputs may be any that keep to these rules, and one draw needn't show every extreme that they name: `face_size`: A face has the same size on both of its slots; the largest face holds all 512 positions and the smallest a quarter of them. `coarse_idx`: the 24 entries of one slot are distinct.
All inputs are finite; a program needn't handle non-finite values.
Results may differ from a plain program's by a relative error of at most 0.0064.
Values sent between devices are 32-bit elements; how exact they have to be, the bound alone decides.
A program may use at most 64 MiB of HBM per device.

v0:
```python
import jax
import jax.numpy as jnp
from jax import lax
from jax.sharding import PartitionSpec as P


def passed_along(shard, axis, by):
    size = lax.axis_size(axis)
    return lax.ppermute(shard, axis, [(i, (i + by) % size) for i in range(size)])


def with_halo(block, sides, width):
    for axis, dim in sides:
        count = lax.axis_size(axis)
        forward = [(i, i + 1) for i in range(count - 1)]
        forward.append((count - 1, 0))
        backward = [(target, source) for source, target in forward]
        low = lax.ppermute(
            lax.slice_in_dim(block, block.shape[dim] - width, None, axis=dim), axis, forward
        )
        high = lax.ppermute(lax.slice_in_dim(block, 0, width, axis=dim), axis, backward)
        block = jnp.concatenate([low, block, high], axis=dim)
    return block


def swap_faces(applied):
    received = {}
    for offset, member in ((-1, 0), (1, 1)):
        received[member] = passed_along(applied[1 - member], "gx", offset)
    for offset, member in ((-1, 2), (1, 3)):
        received[member] = passed_along(applied[5 - member], "gy", offset)
    for offset, member in ((-1, 4), (1, 5)):
        received[member] = passed_along(applied[9 - member], "gz", offset)
    return jnp.stack([received[member] for member in range(6)], axis=0)


def on_device(residual, panel, face_block, deluxe_inv, basis, face_size, coarse_idx, coarse_scale):
    values = residual[0, 0, 0]
    pieces = panel[0, 0, 0]
    blocks = face_block[0, 0, 0]
    inverses = deluxe_inv[0, 0, 0]
    bases = basis[0, 0, 0]
    sizes = face_size[0, 0, 0]
    indices = coarse_idx[0, 0, 0]
    scales = coarse_scale[0, 0, 0]
    width = values.shape[-1]
    owned = scales.shape[0]
    facemask = (jnp.arange(width, dtype=jnp.int32)[None, :] < sizes[:, None]).astype(jnp.float32)
    inner = jnp.einsum("skf,skg->sfg", pieces, pieces, preferred_element_type=jnp.float32)
    schur = (blocks.astype(jnp.float32) - inner).astype(jnp.bfloat16)
    masked = values * facemask[:, None, :].astype(jnp.bfloat16)
    applied = (
        jnp.einsum("srf,sgf->srg", masked, schur, preferred_element_type=jnp.float32)
        * facemask[:, None, :]
    )
    summed = (applied + swap_faces(applied)).astype(jnp.bfloat16)
    averaged = jnp.einsum("srf,sgf->srg", summed, inverses, preferred_element_type=jnp.float32)
    averaged = (averaged * facemask[:, None, :]).astype(jnp.bfloat16)
    partial_value = jnp.einsum("srf,scf->src", averaged, bases, preferred_element_type=jnp.float32)
    columns = jnp.arange(2 * owned, dtype=jnp.int32)
    onehot = (indices[:, :, None] == columns[None, None, :]).astype(jnp.float32)
    split = jnp.einsum("src,scn->srn", partial_value, onehot, precision=lax.Precision.HIGHEST)
    own_terms = jnp.sum(split[:, :, :owned], axis=0)
    outward = split[:, :, owned:][None, None, None]
    rims = with_halo(outward, (("gx", 0), ("gy", 1), ("gz", 2)), 1)
    incoming = (
        rims[0, 1, 1, 0]
        + rims[2, 1, 1, 1]
        + rims[1, 0, 1, 2]
        + rims[1, 2, 1, 3]
        + rims[1, 1, 0, 4]
        + rims[1, 1, 2, 5]
    )
    mine = own_terms + incoming
    correction = mine * scales[None, :]
    beside_all = with_halo(correction[None, None, None], (("gx", 0), ("gy", 1), ("gz", 2)), 1)
    fetched = jnp.stack(
        [
            beside_all[2, 1, 1],
            beside_all[0, 1, 1],
            beside_all[1, 2, 1],
            beside_all[1, 0, 1],
            beside_all[1, 1, 2],
            beside_all[1, 1, 0],
        ],
        axis=0,
    )
    tables = jnp.concatenate([jnp.broadcast_to(correction[None], fetched.shape), fetched], axis=2)
    picked = jnp.einsum("srn,scn->scr", tables, onehot, precision=lax.Precision.HIGHEST)
    added = jnp.einsum(
        "scr,scf->srf", picked, bases.astype(jnp.float32), precision=lax.Precision.HIGHEST
    )
    corrected = (averaged.astype(jnp.float32) + added) * facemask[:, None, :]
    return corrected.astype(jnp.bfloat16)[None, None, None]


def solution(mesh):
    placed = (
        P("gx", "gy", "gz", None, None, None),
        P("gx", "gy", "gz", None, None, None),
        P("gx", "gy", "gz", None, None, None),
        P("gx", "gy", "gz", None, None, None),
        P("gx", "gy", "gz", None, None, None),
        P("gx", "gy", "gz", None),
        P("gx", "gy", "gz", None, None),
        P("gx", "gy", "gz", None),
    )
    return jax.shard_map(
        on_device,
        mesh=mesh,
        in_specs=placed,
        out_specs=P("gx", "gy", "gz", None, None, None),
        check_vma=False,
    )
```

profile of v0, /device:TPU:0, one launch (start us, length us, event | category | flops | bytes accessed | tf_op | source)
XLA Modules:
  0.0 103.6 jit_solution(12045693651157887022)
XLA Ops:
  0.0 1.5 %fusion.40 = (bf16[6,512]{1,0:T(8,128)(2,1)}, f32[6,512]{1,0:T(8,128)S(1)}) fusion(s32[6]{0:T(128)} %bitcast.102), kind=kLoop, calls=%fused_computation.68 | loop fusion | flops 9216 | bytes 18456 | tf_op jit(solution)/shard_map/convert_element_type | solution.py:51
  1.5 10.1 %fusion.12 = f32[6,32,512]{2,1,0:T(8,128)S(1)} fusion(bf16[1,1,1,6,512,512]{5,4,3,2,1,0:T(8,128)(2,1)} %param.10, bf16[1,1,1,6,1024,512]{5,4,3,2,1,0:T(8,128)(2,1)} %param.9, bf16[1,1,1,6,32,512]{5,4,3,2,1,0:T(8,128)(2,1)} %param.8, f32[6,512]{1,0:T(8,128)S(1)} %get-tuple-element.16, bf16[6,512]{1,0:T(8,128)(2,1)} %get-tuple-element.15), kind=kOutput, calls=%fused_computation.8 | convolution fusion | flops 3326803968 | bytes 10045440 | tf_op jit(solution)/shard_map/srf,sgf->srg/dot_general | solution.py:53
  11.6 3.0 %collective-permute-start = (f32[32,512]{1,0:T(8,128)S(1)}, f32[32,512]{1,0:T(8,128)S(1)}, u32[]{:S(2)}, u32[]{:S(2)}) collective-permute-start(f32[32,512]{1,0:T(8,128)S(1)} %get-tuple-element.12), channel_id=1, source_target_pairs={{0,16},{16,0},{1,17},{17,1},{2,18},{18,2},{3,19},{19,3},{4,20},{20... | collective-permute-start | bytes 196616 | tf_op jit(solution)/shard_map/ppermute | solution.py:9
  14.6 1.6 %collective-permute-start.5 = (f32[32,512]{1,0:T(8,128)S(1)}, f32[32,512]{1,0:T(8,128)S(1)}, u32[]{:S(2)}, u32[]{:S(2)}) collective-permute-start(f32[32,512]{1,0:T(8,128)S(1)} %get-tuple-element.7), channel_id=1, source_target_pairs={{0,1},{1,2},{2,3},{3,0},{4,5},{5,6},{6,7},{7,4},{8,9},{9,10},{10,1... | collective-permute-start | bytes 196616 | tf_op jit(solution)/shard_map/ppermute | solution.py:9
  16.2 2.2 %collective-permute-start.4 = (f32[32,512]{1,0:T(8,128)S(1)}, f32[32,512]{1,0:T(8,128)S(1)}, u32[]{:S(2)}, u32[]{:S(2)}) collective-permute-start(f32[32,512]{1,0:T(8,128)S(1)} %get-tuple-element.8), channel_id=1, source_target_pairs={{0,3},{1,0},{2,1},{3,2},{4,7},{5,4},{6,5},{7,6},{8,11},{9,8},{10,9... | collective-permute-start | bytes 196616 | tf_op jit(solution)/shard_map/ppermute | solution.py:9
  18.5 1.7 %collective-permute-start.2 = (f32[32,512]{1,0:T(8,128)S(1)}, f32[32,512]{1,0:T(8,128)S(1)}, u32[]{:S(2)}, u32[]{:S(2)}) collective-permute-start(f32[32,512]{1,0:T(8,128)S(1)} %get-tuple-element.10), channel_id=1, source_target_pairs={{0,12},{4,0},{8,4},{12,8},{1,13},{5,1},{9,5},{13,9},{2,14},{6,2},{... | collective-permute-start | bytes 196616 | tf_op jit(solution)/shard_map/ppermute | solution.py:9
  20.2 0.7 copy.11
  20.9 0.3 collective-permute-start.1
  21.3 3.9 %collective-permute-done.1 = f32[32,512]{1,0:T(8,128)S(1)} collective-permute-done((f32[32,512]{1,0:T(8,128)S(1)}, f32[32,512]{1,0:T(8,128)S(1)}, u32[]{:S(2)}, u32[]{:S(2)}) %collective-permute-start.1) | collective-permute-done | bytes 65568 | tf_op jit(solution)/shard_map/ppermute | solution.py:9
  25.3 1.0 fusion.21
  26.5 0.4 fusion.34
  27.0 0.4 collective-permute-start.7
  27.4 1.7 %collective-permute-start.6 = (f32[1,1,1,6,32,32]{5,4,3,2,1,0:T(8,128)S(1)}, f32[1,1,1,6,32,32]{5,4,3,2,1,0:T(8,128)S(1)}, u32[]{:S(2)}, u32[]{:S(2)}) collective-permute-start(f32[1,1,1,6,32,32]{5,4,3,2,1,0:T(8,128)S(1)} %get-tuple-element.13), channel_id=1, source_target_pairs={{0,16},{16,0},{1,17},{17,1},{2,18},{18,2},{3,19},{19,3},{4,20},{20... | collective-permute-start | bytes 73736 | tf_op jit(solution)/shard_map/ppermute | solution.py:18
  29.0 2.6 %collective-permute-done.7 = f32[1,1,1,6,32,32]{5,4,3,2,1,0:T(8,128)S(1)} collective-permute-done((f32[1,1,1,6,32,32]{5,4,3,2,1,0:T(8,128)S(1)}, f32[1,1,1,6,32,32]{5,4,3,2,1,0:T(8,128)S(1)}, u32[]{:S(2)}, u32[]{:S(2)}) %collective-permute-start.7) | collective-permute-done | bytes 24608 | tf_op jit(solution)/shard_map/ppermute | solution.py:21
  31.6 1.1 %collective-permute-done.6 = f32[1,1,1,6,32,32]{5,4,3,2,1,0:T(8,128)S(1)} collective-permute-done((f32[1,1,1,6,32,32]{5,4,3,2,1,0:T(8,128)S(1)}, f32[1,1,1,6,32,32]{5,4,3,2,1,0:T(8,128)S(1)}, u32[]{:S(2)}, u32[]{:S(2)}) %collective-permute-start.6) | collective-permute-done | bytes 24608 | tf_op jit(solution)/shard_map/ppermute | solution.py:18
  32.8 0.5 collective-permute-start.8
  33.3 5.9 %collective-permute-done.9 = f32[3,1,1,6,32,32]{5,4,3,2,1,0:T(8,128)S(1)} collective-permute-done((f32[3,1,1,6,32,32]{5,4,3,2,1,0:T(8,128)S(1)}, f32[3,1,1,6,32,32]{5,4,3,2,1,0:T(8,128)S(1)}, u32[]{:S(2)}, u32[]{:S(2)}) %collective-permute-start.9) | collective-permute-done | bytes 73760 | tf_op jit(solution)/shard_map/ppermute | solution.py:21
  39.2 3.0 %collective-permute-done.8 = f32[3,1,1,6,32,32]{5,4,3,2,1,0:T(8,128)S(1)} collective-permute-done((f32[3,1,1,6,32,32]{5,4,3,2,1,0:T(8,128)S(1)}, f32[3,1,1,6,32,32]{5,4,3,2,1,0:T(8,128)S(1)}, u32[]{:S(2)}, u32[]{:S(2)}) %collective-permute-start.8) | collective-permute-done | bytes 73760 | tf_op jit(solution)/shard_map/ppermute | solution.py:18
  42.2 1.9 %collective-permute-start.11 = (f32[3,3,1,6,32,32]{5,4,3,2,1,0:T(8,128)S(1)}, f32[3,3,1,6,32,32]{5,4,3,2,1,0:T(8,128)S(1)}, u32[]{:S(2)}, u32[]{:S(2)}) collective-permute-start(f32[3,3,1,6,32,32]{5,4,3,2,1,0:T(8,128)S(1)} %pad_maximum_fusion), channel_id=1, source_target_pairs={{1,0},{2,1},{3,2},{0,3},{5,4},{6,5},{7,6},{4,7},{9,8},{10,9},{11,1... | collective-permute-start | bytes 663560 | tf_op jit(solution)/shard_map/ppermute | solution.py:21
  44.3 20.2 %collective-permute-done.11 = f32[3,3,1,6,32,32]{5,4,3,2,1,0:T(8,128)S(1)} collective-permute-done((f32[3,3,1,6,32,32]{5,4,3,2,1,0:T(8,128)S(1)}, f32[3,3,1,6,32,32]{5,4,3,2,1,0:T(8,128)S(1)}, u32[]{:S(2)}, u32[]{:S(2)}) %collective-permute-start.11) | collective-permute-done | bytes 221216 | tf_op jit(solution)/shard_map/ppermute | solution.py:21
  64.5 18.6 %collective-permute-done.10 = f32[3,3,1,6,32,32]{5,4,3,2,1,0:T(8,128)S(1)} collective-permute-done((f32[3,3,1,6,32,32]{5,4,3,2,1,0:T(8,128)S(1)}, f32[3,3,1,6,32,32]{5,4,3,2,1,0:T(8,128)S(1)}, u32[]{:S(2)}, u32[]{:S(2)}) %collective-permute-start.10) | collective-permute-done | bytes 221216 | tf_op jit(solution)/shard_map/ppermute | solution.py:18
  83.2 1.0 %collective-permute-start.13 = (f32[1,1,1,32,32]{4,3,2,1,0:T(8,128)S(1)}, f32[1,1,1,32,32]{4,3,2,1,0:T(8,128)S(1)}, u32[]{:S(2)}, u32[]{:S(2)}) collective-permute-start(f32[1,1,1,32,32]{4,3,2,1,0:T(8,128)S(1)} %fusion.37), channel_id=1, source_target_pairs={{0,16},{16,0},{1,17},{17,1},{2,18},{18,2},{3,19},{19,3},{4,20},{20... | collective-permute-start | bytes 12296 | tf_op jit(solution)/shard_map/ppermute | solution.py:18
  84.2 1.1 %collective-permute-start.12 = (f32[1,1,1,32,32]{4,3,2,1,0:T(8,128)S(1)}, f32[1,1,1,32,32]{4,3,2,1,0:T(8,128)S(1)}, u32[]{:S(2)}, u32[]{:S(2)}) collective-permute-start(f32[1,1,1,32,32]{4,3,2,1,0:T(8,128)S(1)} %fusion.37), channel_id=1, source_target_pairs={{16,0},{0,16},{17,1},{1,17},{18,2},{2,18},{19,3},{3,19},{20,4},{4,... | collective-permute-start | bytes 12296 | tf_op jit(solution)/shard_map/ppermute | solution.py:21
  85.3 1.7 %collective-permute-done.13 = f32[1,1,1,32,32]{4,3,2,1,0:T(8,128)S(1)} collective-permute-done((f32[1,1,1,32,32]{4,3,2,1,0:T(8,128)S(1)}, f32[1,1,1,32,32]{4,3,2,1,0:T(8,128)S(1)}, u32[]{:S(2)}, u32[]{:S(2)}) %collective-permute-start.13) | collective-permute-done | bytes 4128 | tf_op jit(solution)/shard_map/ppermute | solution.py:18
  87.0 1.0 collective-permute-done.12
  88.0 1.7 %collective-permute-start.14 = (f32[3,1,1,32,32]{4,3,2,1,0:T(8,128)S(1)}, f32[3,1,1,32,32]{4,3,2,1,0:T(8,128)S(1)}, u32[]{:S(2)}, u32[]{:S(2)}) collective-permute-start(f32[3,1,1,32,32]{4,3,2,1,0:T(8,128)S(1)} %pad_maximum_fusion.3), channel_id=1, source_target_pairs={{4,0},{8,4},{12,8},{0,12},{5,1},{9,5},{13,9},{1,13},{6,2},{10,6},{... | collective-permute-start | bytes 36872 | tf_op jit(solution)/shard_map/ppermute | solution.py:21
  89.8 2.1 %collective-permute-done.15 = f32[3,1,1,32,32]{4,3,2,1,0:T(8,128)S(1)} collective-permute-done((f32[3,1,1,32,32]{4,3,2,1,0:T(8,128)S(1)}, f32[3,1,1,32,32]{4,3,2,1,0:T(8,128)S(1)}, u32[]{:S(2)}, u32[]{:S(2)}) %collective-permute-start.15) | collective-permute-done | bytes 12320 | tf_op jit(solution)/shard_map/ppermute | solution.py:18
  91.9 1.7 %collective-permute-start.17 = (f32[3,3,1,32,32]{4,3,2,1,0:T(8,128)S(1)}, f32[3,3,1,32,32]{4,3,2,1,0:T(8,128)S(1)}, u32[]{:S(2)}, u32[]{:S(2)}) collective-permute-start(f32[3,3,1,32,32]{4,3,2,1,0:T(8,128)S(1)} %pad_maximum_fusion.2), channel_id=1, source_target_pairs={{0,1},{1,2},{2,3},{3,0},{4,5},{5,6},{6,7},{7,4},{8,9},{9,10},{10,1... | collective-permute-start | bytes 110600 | tf_op jit(solution)/shard_map/ppermute | solution.py:18
  93.6 2.2 %collective-permute-start.16 = (f32[3,3,1,32,32]{4,3,2,1,0:T(8,128)S(1)}, f32[3,3,1,32,32]{4,3,2,1,0:T(8,128)S(1)}, u32[]{:S(2)}, u32[]{:S(2)}) collective-permute-start(f32[3,3,1,32,32]{4,3,2,1,0:T(8,128)S(1)} %pad_maximum_fusion.2), channel_id=1, source_target_pairs={{1,0},{2,1},{3,2},{0,3},{5,4},{6,5},{7,6},{4,7},{9,8},{10,9},{11,1... | collective-permute-start | bytes 110600 | tf_op jit(solution)/shard_map/ppermute | solution.py:21
  95.8 6.4 %collective-permute-done.16 = f32[3,3,1,32,32]{4,3,2,1,0:T(8,128)S(1)} collective-permute-done((f32[3,3,1,32,32]{4,3,2,1,0:T(8,128)S(1)}, f32[3,3,1,32,32]{4,3,2,1,0:T(8,128)S(1)}, u32[]{:S(2)}, u32[]{:S(2)}) %collective-permute-start.16) | collective-permute-done | bytes 36896 | tf_op jit(solution)/shard_map/ppermute | solution.py:21
  102.2 0.3 fusion.29
  102.5 1.1 %fusion.25 = bf16[1,1,1,6,32,512]{5,4,3,2,1,0:T(8,128)(2,1)} fusion(f32[6,24,32]{2,1,0:T(8,128)S(1)} %fusion.29, bf16[6,32,512]{2,1,0:T(8,128)(2,1)S(1)} %fusion.21, f32[6,512]{1,0:T(8,128)S(1)} %get-tuple-element.16, bf16[1,1,1,6,24,512]{5,4,3,2,1,0:T(8,128)(2,1)S(1)} %copy-done.1), kind=kOutput, calls=%fused_computation.14 | convolution fusion | flops 28704768 | bytes 571392 | tf_op jit(solution)/shard_map/scr,scf->srf/dot_general | solution.py:90
  (39 shorter events, 0.9 us)
Async XLA Ops:
  0.0 25.3 %copy-start = (bf16[1,1,1,6,512,512]{5,4,3,2,1,0:T(8,128)(2,1)S(1)}, bf16[1,1,1,6,512,512]{5,4,3,2,1,0:T(8,128)(2,1)}, u32[]{:S(2)}) copy-start(bf16[1,1,1,6,512,512]{5,4,3,2,1,0:T(8,128)(2,1)} %param.11) | copy-start | bytes 9437188
  11.6 14.7 %copy-start.1 = (bf16[1,1,1,6,24,512]{5,4,3,2,1,0:T(8,128)(2,1)S(1)}, bf16[1,1,1,6,24,512]{5,4,3,2,1,0:T(8,128)(2,1)}, u32[]{:S(2)}) copy-start(bf16[1,1,1,6,24,512]{5,4,3,2,1,0:T(8,128)(2,1)} %param.12) | copy-start | bytes 442372
  11.6 9.3 %collective-permute-start = (f32[32,512]{1,0:T(8,128)S(1)}, f32[32,512]{1,0:T(8,128)S(1)}, u32[]{:S(2)}, u32[]{:S(2)}) collective-permute-start(f32[32,512]{1,0:T(8,128)S(1)} %get-tuple-element.12), channel_id=1, source_target_pairs={{0,16},{16,0},{1,17},{17,1},{2,18},{18,2},{3,19},{19,3},{4,20},{20... | collective-permute-start | bytes 196616 | tf_op jit(solution)/shard_map/ppermute | solution.py:9
  14.6 10.6 %collective-permute-start.5 = (f32[32,512]{1,0:T(8,128)S(1)}, f32[32,512]{1,0:T(8,128)S(1)}, u32[]{:S(2)}, u32[]{:S(2)}) collective-permute-start(f32[32,512]{1,0:T(8,128)S(1)} %get-tuple-element.7), channel_id=1, source_target_pairs={{0,1},{1,2},{2,3},{3,0},{4,5},{5,6},{6,7},{7,4},{8,9},{9,10},{10,1... | collective-permute-start | bytes 196616 | tf_op jit(solution)/shard_map/ppermute | solution.py:9
  16.2 9.0 %collective-permute-start.4 = (f32[32,512]{1,0:T(8,128)S(1)}, f32[32,512]{1,0:T(8,128)S(1)}, u32[]{:S(2)}, u32[]{:S(2)}) collective-permute-start(f32[32,512]{1,0:T(8,128)S(1)} %get-tuple-element.8), channel_id=1, source_target_pairs={{0,3},{1,0},{2,1},{3,2},{4,7},{5,4},{6,5},{7,6},{8,11},{9,8},{10,9... | collective-permute-start | bytes 196616 | tf_op jit(solution)/shard_map/ppermute | solution.py:9
  18.5 6.7 %collective-permute-start.3 = (f32[32,512]{1,0:T(8,128)S(1)}, f32[32,512]{1,0:T(8,128)S(1)}, u32[]{:S(2)}, u32[]{:S(2)}) collective-permute-start(f32[32,512]{1,0:T(8,128)S(1)} %get-tuple-element.9), channel_id=1, source_target_pairs={{0,4},{4,8},{8,12},{12,0},{1,5},{5,9},{9,13},{13,1},{2,6},{6,10},{... | collective-permute-start | bytes 196616 | tf_op jit(solution)/shard_map/ppermute | solution.py:9
  18.5 6.7 %collective-permute-start.2 = (f32[32,512]{1,0:T(8,128)S(1)}, f32[32,512]{1,0:T(8,128)S(1)}, u32[]{:S(2)}, u32[]{:S(2)}) collective-permute-start(f32[32,512]{1,0:T(8,128)S(1)} %get-tuple-element.10), channel_id=1, source_target_pairs={{0,12},{4,0},{8,4},{12,8},{1,13},{5,1},{9,5},{13,9},{2,14},{6,2},{... | collective-permute-start | bytes 196616 | tf_op jit(solution)/shard_map/ppermute | solution.py:9
  20.9 4.3 %collective-permute-start.1 = (f32[32,512]{1,0:T(8,128)S(1)}, f32[32,512]{1,0:T(8,128)S(1)}, u32[]{:S(2)}, u32[]{:S(2)}) collective-permute-start(f32[32,512]{1,0:T(8,128)S(1)} %get-tuple-element.11), channel_id=1, source_target_pairs={{0,16},{16,0},{1,17},{17,1},{2,18},{18,2},{3,19},{19,3},{4,20},{20... | collective-permute-start | bytes 196616 | tf_op jit(solution)/shard_map/ppermute | solution.py:9
  25.3 57.9 %copy-start.2 = (f32[1,1,1,32]{3,2,1,0:T(1,128)S(1)}, f32[1,1,1,32]{3,2,1,0:T(1,128)}, u32[]{:S(2)}) copy-start(f32[1,1,1,32]{3,2,1,0:T(1,128)} %param.15) | copy-start | bytes 388
  27.0 4.7 %collective-permute-start.7 = (f32[1,1,1,6,32,32]{5,4,3,2,1,0:T(8,128)S(1)}, f32[1,1,1,6,32,32]{5,4,3,2,1,0:T(8,128)S(1)}, u32[]{:S(2)}, u32[]{:S(2)}) collective-permute-start(f32[1,1,1,6,32,32]{5,4,3,2,1,0:T(8,128)S(1)} %get-tuple-element.13), channel_id=1, source_target_pairs={{16,0},{0,16},{17,1},{1,17},{18,2},{2,18},{19,3},{3,19},{20,4},{4,... | collective-permute-start | bytes 73736 | tf_op jit(solution)/shard_map/ppermute | solution.py:21
  27.4 5.3 %collective-permute-start.6 = (f32[1,1,1,6,32,32]{5,4,3,2,1,0:T(8,128)S(1)}, f32[1,1,1,6,32,32]{5,4,3,2,1,0:T(8,128)S(1)}, u32[]{:S(2)}, u32[]{:S(2)}) collective-permute-start(f32[1,1,1,6,32,32]{5,4,3,2,1,0:T(8,128)S(1)} %get-tuple-element.13), channel_id=1, source_target_pairs={{0,16},{16,0},{1,17},{17,1},{2,18},{18,2},{3,19},{19,3},{4,20},{20... | collective-permute-start | bytes 73736 | tf_op jit(solution)/shard_map/ppermute | solution.py:18
  32.7 6.5 %collective-permute-start.9 = (f32[3,1,1,6,32,32]{5,4,3,2,1,0:T(8,128)S(1)}, f32[3,1,1,6,32,32]{5,4,3,2,1,0:T(8,128)S(1)}, u32[]{:S(2)}, u32[]{:S(2)}) collective-permute-start(f32[3,1,1,6,32,32]{5,4,3,2,1,0:T(8,128)S(1)} %pad_maximum_fusion.1), channel_id=1, source_target_pairs={{4,0},{8,4},{12,8},{0,12},{5,1},{9,5},{13,9},{1,13},{6,2},{10,6},{... | collective-permute-start | bytes 221192 | tf_op jit(solution)/shard_map/ppermute | solution.py:21
  32.8 9.3 %collective-permute-start.8 = (f32[3,1,1,6,32,32]{5,4,3,2,1,0:T(8,128)S(1)}, f32[3,1,1,6,32,32]{5,4,3,2,1,0:T(8,128)S(1)}, u32[]{:S(2)}, u32[]{:S(2)}) collective-permute-start(f32[3,1,1,6,32,32]{5,4,3,2,1,0:T(8,128)S(1)} %pad_maximum_fusion.1), channel_id=1, source_target_pairs={{0,4},{4,8},{8,12},{12,0},{1,5},{5,9},{9,13},{13,1},{2,6},{6,10},{... | collective-permute-start | bytes 221192 | tf_op jit(solution)/shard_map/ppermute | solution.py:18
  42.2 22.3 %collective-permute-start.11 = (f32[3,3,1,6,32,32]{5,4,3,2,1,0:T(8,128)S(1)}, f32[3,3,1,6,32,32]{5,4,3,2,1,0:T(8,128)S(1)}, u32[]{:S(2)}, u32[]{:S(2)}) collective-permute-start(f32[3,3,1,6,32,32]{5,4,3,2,1,0:T(8,128)S(1)} %pad_maximum_fusion), channel_id=1, source_target_pairs={{1,0},{2,1},{3,2},{0,3},{5,4},{6,5},{7,6},{4,7},{9,8},{10,9},{11,1... | collective-permute-start | bytes 663560 | tf_op jit(solution)/shard_map/ppermute | solution.py:21
  44.1 39.1 %collective-permute-start.10 = (f32[3,3,1,6,32,32]{5,4,3,2,1,0:T(8,128)S(1)}, f32[3,3,1,6,32,32]{5,4,3,2,1,0:T(8,128)S(1)}, u32[]{:S(2)}, u32[]{:S(2)}) collective-permute-start(f32[3,3,1,6,32,32]{5,4,3,2,1,0:T(8,128)S(1)} %pad_maximum_fusion), channel_id=1, source_target_pairs={{0,1},{1,2},{2,3},{3,0},{4,5},{5,6},{6,7},{7,4},{8,9},{9,10},{10,1... | collective-permute-start | bytes 663560 | tf_op jit(solution)/shard_map/ppermute | solution.py:18
  83.2 3.8 %collective-permute-start.13 = (f32[1,1,1,32,32]{4,3,2,1,0:T(8,128)S(1)}, f32[1,1,1,32,32]{4,3,2,1,0:T(8,128)S(1)}, u32[]{:S(2)}, u32[]{:S(2)}) collective-permute-start(f32[1,1,1,32,32]{4,3,2,1,0:T(8,128)S(1)} %fusion.37), channel_id=1, source_target_pairs={{0,16},{16,0},{1,17},{17,1},{2,18},{18,2},{3,19},{19,3},{4,20},{20... | collective-permute-start | bytes 12296 | tf_op jit(solution)/shard_map/ppermute | solution.py:18
  84.2 3.7 %collective-permute-start.12 = (f32[1,1,1,32,32]{4,3,2,1,0:T(8,128)S(1)}, f32[1,1,1,32,32]{4,3,2,1,0:T(8,128)S(1)}, u32[]{:S(2)}, u32[]{:S(2)}) collective-permute-start(f32[1,1,1,32,32]{4,3,2,1,0:T(8,128)S(1)} %fusion.37), channel_id=1, source_target_pairs={{16,0},{0,16},{17,1},{1,17},{18,2},{2,18},{19,3},{3,19},{20,4},{4,... | collective-permute-start | bytes 12296 | tf_op jit(solution)/shard_map/ppermute | solution.py:21
  88.0 3.9 %collective-permute-start.15 = (f32[3,1,1,32,32]{4,3,2,1,0:T(8,128)S(1)}, f32[3,1,1,32,32]{4,3,2,1,0:T(8,128)S(1)}, u32[]{:S(2)}, u32[]{:S(2)}) collective-permute-start(f32[3,1,1,32,32]{4,3,2,1,0:T(8,128)S(1)} %pad_maximum_fusion.3), channel_id=1, source_target_pairs={{0,4},{4,8},{8,12},{12,0},{1,5},{5,9},{9,13},{13,1},{2,6},{6,10},{... | collective-permute-start | bytes 36872 | tf_op jit(solution)/shard_map/ppermute | solution.py:18
  88.0 3.9 %collective-permute-start.14 = (f32[3,1,1,32,32]{4,3,2,1,0:T(8,128)S(1)}, f32[3,1,1,32,32]{4,3,2,1,0:T(8,128)S(1)}, u32[]{:S(2)}, u32[]{:S(2)}) collective-permute-start(f32[3,1,1,32,32]{4,3,2,1,0:T(8,128)S(1)} %pad_maximum_fusion.3), channel_id=1, source_target_pairs={{4,0},{8,4},{12,8},{0,12},{5,1},{9,5},{13,9},{1,13},{6,2},{10,6},{... | collective-permute-start | bytes 36872 | tf_op jit(solution)/shard_map/ppermute | solution.py:21
  91.9 10.3 %collective-permute-start.17 = (f32[3,3,1,32,32]{4,3,2,1,0:T(8,128)S(1)}, f32[3,3,1,32,32]{4,3,2,1,0:T(8,128)S(1)}, u32[]{:S(2)}, u32[]{:S(2)}) collective-permute-start(f32[3,3,1,32,32]{4,3,2,1,0:T(8,128)S(1)} %pad_maximum_fusion.2), channel_id=1, source_target_pairs={{0,1},{1,2},{2,3},{3,0},{4,5},{5,6},{6,7},{7,4},{8,9},{9,10},{10,1... | collective-permute-start | bytes 110600 | tf_op jit(solution)/shard_map/ppermute | solution.py:18
  93.6 8.6 %collective-permute-start.16 = (f32[3,3,1,32,32]{4,3,2,1,0:T(8,128)S(1)}, f32[3,3,1,32,32]{4,3,2,1,0:T(8,128)S(1)}, u32[]{:S(2)}, u32[]{:S(2)}) collective-permute-start(f32[3,3,1,32,32]{4,3,2,1,0:T(8,128)S(1)} %pad_maximum_fusion.2), channel_id=1, source_target_pairs={{1,0},{2,1},{3,2},{0,3},{5,4},{6,5},{7,6},{4,7},{9,8},{10,9},{11,1... | collective-permute-start | bytes 110600 | tf_op jit(solution)/shard_map/ppermute | solution.py:21
where the time goes:
time: 104 us
  waiting for transfers between devices  66.5 us (64%)
  starting transfers between devices  21.4 us (21%)
  matrix products  13 us (12%)
  other arithmetic  1.71 us (2%)
    ppermute x6, waiting for transfers between devices, with_halo(): lax.ppermute(lax.slice_in_dim(block, 0, width, axis=dim), axis, backward)  36.1 us
    ppermute x6, waiting for transfers between devices, with_halo(): lax.ppermute(lax.slice_in_dim(block, block.shape[dim] - width, None, axis...  26.5 us
    dot_general x1, matrix products, on_device(): jnp.einsum('srf,sgf->srg', masked, schur, preferred_element_type=jnp.floa...  10.1 us
    ppermute x6, starting transfers between devices, passed_along(): lax.ppermute(shard, axis, [(i, (i + by) % size) for i in range(size)])  8.92 us
    ppermute x6, starting transfers between devices, with_halo(): lax.ppermute(lax.slice_in_dim(block, 0, width, axis=dim), axis, backward)  7.31 us
    ppermute x6, starting transfers between devices, with_halo(): lax.ppermute(lax.slice_in_dim(block, block.shape[dim] - width, None, axis...  5.16 us
    ppermute x6, waiting for transfers between devices, passed_along(): lax.ppermute(shard, axis, [(i, (i + by) % size) for i in range(size)])  3.93 us
  transfers between devices with their start and end apart: 18, of which 11 were waited for; matrix products, arithmetic and copies ran while one was open for 1% of the time, Pallas kernels for 0%

commit v1 on v0

v1 whole, which is shorter than its diff:
```python
import functools

import jax
import jax.numpy as jnp
from jax import lax
from jax.experimental import pallas as pl
from jax.experimental.pallas import tpu as pltpu
from jax.sharding import PartitionSpec as P

AXES = ("gx", "gy", "gz")
ORDER = (0, 1, 4, 5, 2, 3)
MESH = pl.DeviceIdType.MESH
F32 = jnp.float32
BF16 = jnp.bfloat16


def dot_nt(a, b):
    return lax.dot_general(a, b, (((1,), (1,)), ((), ())), preferred_element_type=F32)


def dot_nn(a, b):
    return lax.dot_general(a, b, (((1,), (0,)), ((), ())), preferred_element_type=F32)


def kernel(
    sizes,
    residual, panel, face_block, deluxe_inv, basis, size_ref, idx_ref, scale_ref,
    out_ref,
    res_v, pan_v, fb_v, inv_v, bas_v, size_s, idx_v, scale_v,
    expanded, applied, recv1, averaged, send2, recv2, send3, recv3,
    sem_res, sem_pan, sem_fb, sem_inv, sem_bas, sem_small,
    ssem1, rsem1, ssem2, rsem2, ssem3, rsem3,
):
    me = [lax.axis_index(name) for name in AXES]

    def neighbour(slot):
        axis = slot // 2
        step = 1 if slot % 2 == 0 else sizes[axis] - 1
        coords = list(me)
        coords[axis] = lax.rem(me[axis] + step, sizes[axis])
        return tuple(coords)

    barrier = pltpu.get_barrier_semaphore()
    for slot in range(6):
        pl.semaphore_signal(barrier, inc=1, device_id=neighbour(slot), device_id_type=MESH)

    def remote(src, dst, ssem, rsem, slot):
        return pltpu.make_async_remote_copy(
            src_ref=src.at[slot] if src.shape[0] == 6 else src.at[0],
            dst_ref=dst.at[slot ^ 1],
            send_sem=ssem.at[slot],
            recv_sem=rsem.at[slot ^ 1],
            device_id=neighbour(slot),
            device_id_type=MESH,
        )

    c_size = pltpu.make_async_copy(size_ref.at[0, 0], size_s, sem_small.at[0])
    c_idx = pltpu.make_async_copy(idx_ref.at[0, 0, 0], idx_v, sem_small.at[1])
    c_scale = pltpu.make_async_copy(scale_ref.at[0, 0], scale_v, sem_small.at[2])
    c_res = pltpu.make_async_copy(residual.at[0, 0, 0], res_v, sem_res)
    c_bas = pltpu.make_async_copy(basis.at[0, 0, 0], bas_v, sem_bas)
    c_pan = [pltpu.make_async_copy(panel.at[0, 0, 0, s], pan_v.at[s], sem_pan.at[s]) for s in range(6)]
    c_fb = [pltpu.make_async_copy(face_block.at[0, 0, 0, s], fb_v.at[s], sem_fb.at[s]) for s in range(6)]
    c_inv = [pltpu.make_async_copy(deluxe_inv.at[0, 0, 0, s], inv_v.at[s], sem_inv.at[s]) for s in range(6)]
    for copy in (c_size, c_idx, c_scale, c_res, c_bas):
        copy.start()
    for s in ORDER:
        c_pan[s].start()
        c_fb[s].start()
    for s in ORDER:
        c_inv[s].start()

    width = res_v.shape[-1]
    lane = lax.broadcasted_iota(jnp.int32, (1, width), 1)
    c_size.wait()
    live = [lane < size_s[0, s] for s in range(6)]

    c_idx.wait()
    c_bas.wait()
    row = lax.broadcasted_iota(jnp.int32, (256, 1), 0)
    unknown = (row & 31) + 32 * (row >> 7)
    for s in ORDER:
        onehot = jnp.where(unknown == idx_v[pl.ds(s, 1), :], 1.0, 0.0).astype(BF16)
        expanded[s] = dot_nn(onehot, bas_v[s]).astype(BF16)

    c_res.wait()
    for k, s in enumerate(ORDER):
        c_pan[s].wait()
        masked = jnp.where(live[s], res_v[s].astype(F32), 0.0).astype(BF16)
        inner = dot_nt(masked, pan_v[s]).astype(BF16)
        through = dot_nn(inner, pan_v[s])
        c_fb[s].wait()
        value = dot_nt(masked, fb_v[s]) - through
        applied[s] = jnp.where(live[s], value, 0.0)
        if k == 0:
            pl.semaphore_wait(barrier, 6)
        remote(applied, recv1, ssem1, rsem1, s).start()

    group8 = lax.broadcasted_iota(jnp.int32, (8, 128), 1) >> 5

    def packed(wide):
        total = jnp.where(group8 == 0, wide[0:8], 0.0)
        for j in range(1, 4):
            total = jnp.where(group8 == j, wide[8 * j:8 * j + 8], total)
        return total

    def spread(tile):
        return jnp.concatenate([jnp.where(group8 == j, tile, 0.0) for j in range(4)], axis=0)

    own = jnp.zeros((8, 128), F32)
    for s in ORDER:
        remote(applied, recv1, ssem1, rsem1, s ^ 1).wait_recv()
        c_inv[s].wait()
        summed = (applied[s] + recv1[s]).astype(BF16)
        value = jnp.where(live[s], dot_nt(summed, inv_v[s]), 0.0).astype(BF16)
        averaged[s] = value
        split = dot_nt(value, expanded[s])
        own = own + packed(split[:, 0:128])
        send2[s] = packed(split[:, 128:256])
        remote(send2, recv2, ssem2, rsem2, s).start()

    c_scale.wait()
    scale = jnp.concatenate([scale_v[...]] * 4, axis=1)
    for s in ORDER:
        remote(send2, recv2, ssem2, rsem2, s ^ 1).wait_recv()
        own = own + recv2[s]
    correction = own * scale
    send3[0] = correction
    for s in ORDER:
        remote(send3, recv3, ssem3, rsem3, s).start()

    def halves(tile):
        high = tile.astype(BF16)
        return high, (tile - high.astype(F32)).astype(BF16)

    mine = spread(correction)
    for s in ORDER:
        remote(send3, recv3, ssem3, rsem3, s ^ 1).wait_recv()
        table = jnp.concatenate([mine, spread(recv3[s])], axis=1)
        high, low = halves(table)
        added = dot_nn(high, expanded[s]) + dot_nn(low, expanded[s])
        out_ref[0, 0, 0, s] = jnp.where(live[s], averaged[s].astype(F32) + added, 0.0).astype(BF16)

    for s in ORDER:
        remote(applied, recv1, ssem1, rsem1, s).wait_send()
        remote(send2, recv2, ssem2, rsem2, s).wait_send()
        remote(send3, recv3, ssem3, rsem3, s).wait_send()


def on_device(sizes, residual, panel, face_block, deluxe_inv, basis, face_size, coarse_idx, coarse_scale):
    slots, rows, width = residual.shape[3:]
    depth = panel.shape[4]
    entries = basis.shape[4]
    owned = coarse_scale.shape[-1]
    dma = pltpu.SemaphoreType.DMA
    return pl.pallas_call(
        functools.partial(kernel, sizes),
        out_shape=jax.ShapeDtypeStruct(residual.shape, BF16),
        in_specs=[pl.BlockSpec(memory_space=pl.ANY)] * 8,
        out_specs=pl.BlockSpec(memory_space=pltpu.VMEM),
        scratch_shapes=[
            pltpu.VMEM((slots, rows, width), BF16),
            pltpu.VMEM((slots, depth, width), BF16),
            pltpu.VMEM((slots, width, width), BF16),
            pltpu.VMEM((slots, width, width), BF16),
            pltpu.VMEM((slots, entries, width), BF16),
            pltpu.SMEM((1, slots), jnp.int32),
            pltpu.VMEM((slots, entries), jnp.int32),
            pltpu.VMEM((1, owned), F32),
            pltpu.VMEM((slots, 8 * owned, width), BF16),
            pltpu.VMEM((slots, rows, width), F32),
            pltpu.VMEM((slots, rows, width), F32),
            pltpu.VMEM((slots, rows, width), BF16),
            pltpu.VMEM((slots, 8, 128), F32),
            pltpu.VMEM((slots, 8, 128), F32),
            pltpu.VMEM((1, 8, 128), F32),
            pltpu.VMEM((slots, 8, 128), F32),
            dma, dma((6,)), dma((6,)), dma((6,)), dma, dma((3,)),
            dma((6,)), dma((6,)), dma((6,)), dma((6,)), dma((6,)), dma((6,)),
        ],
        compiler_params=pltpu.CompilerParams(
            collective_id=0, has_side_effects=True, vmem_limit_bytes=40 * 1024 * 1024
        ),
    )(residual, panel, face_block, deluxe_inv, basis, face_size, coarse_idx, coarse_scale)


def solution(mesh):
    placed = (
        P("gx", "gy", "gz", None, None, None),
        P("gx", "gy", "gz", None, None, None),
        P("gx", "gy", "gz", None, None, None),
        P("gx", "gy", "gz", None, None, None),
        P("gx", "gy", "gz", None, None, None),
        P("gx", "gy", "gz", None),
        P("gx", "gy", "gz", None, None),
        P("gx", "gy", "gz", None),
    )
    sizes = tuple(mesh.shape[name] for name in AXES)
    return jax.shard_map(
        functools.partial(on_device, sizes),
        mesh=mesh,
        in_specs=placed,
        out_specs=P("gx", "gy", "gz", None, None, None),
        check_vma=False,
    )
```

time: 104 us -> 32.5 us (0.31)
  waiting for transfers between devices: 66.5 us -> 0 us
  starting transfers between devices: 21.4 us -> 0 us
  Pallas kernels: 0 us -> 21.1 us
  matrix products: 13 us -> 0 us
  local copies, waits for them, and re-layouts: 0.79 us -> 11.1 us
  other arithmetic: 1.71 us -> 0 us
    ppermute x18 -> x0, waiting for transfers between devices: 66.5 us -> none  [the longest x6 36.1 us: with_halo(): lax.ppermute(lax.slice_in_dim(block, 0, width, axis=dim), axis, backward)]
    ppermute x18 -> x0, starting transfers between devices: 21.4 us -> none  [the longest x6 8.92 us: passed_along(): lax.ppermute(shard, axis, [(i, (i + by) % size) for i in range(size)])]
    pallas_call x0 -> x1, Pallas kernels: none -> 21.1 us  [on_device(): pl.pallas_call(functools.partial(kernel, sizes), out_shape=jax.ShapeDtype...]
    dot_general x6 -> x0, matrix products: 13 us -> none  [the longest x1 10.1 us: on_device(): jnp.einsum('srf,sgf->srg', masked, schur, preferred_element_type=jnp.floa...]
    unnamed x17 -> x16, local copies, waits for them, and re-layouts: 0.75 us -> 11.1 us
    convert_element_type x1 -> x0, other arithmetic: 1.47 us -> none  [on_device(): masked = values * facemask[:, None, :].astype(jnp.bfloat16)]
  transfers between devices with their start and end apart: 18 -> 0, of which waited for: 11 -> 0; matrix products, arithmetic and copies ran while one was open for 1% -> 0% of each run, Pallas kernels for 0% -> 0%
where the time goes in v1:
time: 32.5 us; the launch traced here: 32.2 us
  Pallas kernels  21.1 us (65%)
  local copies, waits for them, and re-layouts  11.1 us (34%)
    pallas_call x1, Pallas kernels, on_device(): pl.pallas_call(functools.partial(kernel, sizes), out_shape=jax.ShapeDtype...  21.1 us
    unnamed x16, local copies, waits for them, and re-layouts  11.1 us

profile of v1, /device:TPU:0, one launch (start us, length us, event | category | flops | bytes accessed | tf_op | source)
XLA Modules:
  0.0 32.2 jit_solution(12541214724610242906)
XLA Ops:
  0.0 0.7 %copy.9.idx_ref = s32[1,1,1,6,24]{4,3,2,1,0:T(8,128)S(1)} copy(s32[1,1,1,6,24]{4,2,3,1,0:T(1,128)} %param.14) | data formatting | bytes 1152 | tf_op args[6]
  0.7 0.0 copy-start
  0.7 2.8 %copy-done = bf16[1,1,1,6,1024,512]{5,4,3,2,1,0:T(8,128)(2,1)S(1)} copy-done((bf16[1,1,1,6,1024,512]{5,4,3,2,1,0:T(8,128)(2,1)S(1)}, bf16[1,1,1,6,1024,512]{5,4,3,2,1,0:T(8,128)(2,1)}, u32[]{:S(2)}) %copy-start) | copy-done | bytes 6291480
  3.5 0.0 copy-start.1
  3.5 1.9 %copy-done.1 = bf16[1,1,1,6,512,512]{5,4,3,2,1,0:T(8,128)(2,1)S(1)} copy-done((bf16[1,1,1,6,512,512]{5,4,3,2,1,0:T(8,128)(2,1)S(1)}, bf16[1,1,1,6,512,512]{5,4,3,2,1,0:T(8,128)(2,1)}, u32[]{:S(2)}) %copy-start.1) | copy-done | bytes 3145752
  5.4 0.0 copy-start.2
  5.4 1.9 %copy-done.2 = bf16[1,1,1,6,512,512]{5,4,3,2,1,0:T(8,128)(2,1)S(1)} copy-done((bf16[1,1,1,6,512,512]{5,4,3,2,1,0:T(8,128)(2,1)S(1)}, bf16[1,1,1,6,512,512]{5,4,3,2,1,0:T(8,128)(2,1)}, u32[]{:S(2)}) %copy-start.2) | copy-done | bytes 3145752
  7.3 0.0 copy-start.3
  7.3 0.9 %copy-done.3 = bf16[1,1,1,6,32,512]{5,4,3,2,1,0:T(8,128)(2,1)S(1)} copy-done((bf16[1,1,1,6,32,512]{5,4,3,2,1,0:T(8,128)(2,1)S(1)}, bf16[1,1,1,6,32,512]{5,4,3,2,1,0:T(8,128)(2,1)}, u32[]{:S(2)}) %copy-start.3) | copy-done | bytes 196632
  8.2 0.0 copy-start.4
  8.2 0.9 %copy-done.4 = bf16[1,1,1,6,24,512]{5,4,3,2,1,0:T(8,128)(2,1)S(1)} copy-done((bf16[1,1,1,6,24,512]{5,4,3,2,1,0:T(8,128)(2,1)S(1)}, bf16[1,1,1,6,24,512]{5,4,3,2,1,0:T(8,128)(2,1)}, u32[]{:S(2)}) %copy-start.4) | copy-done | bytes 147480
  9.1 0.0 copy-start.5
  9.1 0.7 %copy-done.5 = s32[1,1,1,6]{3,2,1,0:T(1,128)S(1)} copy-done((s32[1,1,1,6]{3,2,1,0:T(1,128)S(1)}, s32[1,1,1,6]{3,2,1,0:T(1,128)}, u32[]{:S(2)}) %copy-start.5) | copy-done | bytes 48
  9.7 0.0 copy-start.6
  9.7 0.7 %copy-done.6 = f32[1,1,1,32]{3,2,1,0:T(1,128)S(1)} copy-done((f32[1,1,1,32]{3,2,1,0:T(1,128)S(1)}, f32[1,1,1,32]{3,2,1,0:T(1,128)}, u32[]{:S(2)}) %copy-start.6) | copy-done | bytes 152
  10.4 21.1 %shard_map.82 = bf16[1,1,1,6,32,512]{5,4,3,2,1,0:T(8,128)(2,1)S(1)} custom-call(bf16[1,1,1,6,32,512]{5,4,3,2,1,0:T(8,128)(2,1)S(1)} %copy-done.3, bf16[1,1,1,6,1024,512]{5,4,3,2,1,0:T(8,128)(2,1)S(1)} %copy-done, bf16[1,1,1,6,512,512]{5,4,3,2,1,0:T(8,128)(2,1)S(1)} %copy-done.1, bf16[1,1,1,6,512,512]{5,4,3,2,1,0:T(8,128)(2,1)S(1)} %copy-done.2, ...), custom_call_target="tpu_custom_call" | custom-call | tf_op jit(solution)/shard_map/pallas_call | solution.py:156
  31.5 0.7 %copy.11 = bf16[1,1,1,6,32,512]{5,4,3,2,1,0:T(8,128)(2,1)} copy(bf16[1,1,1,6,32,512]{5,4,3,2,1,0:T(8,128)(2,1)S(1)} %shard_map.82) | data formatting | bytes 393216
Async XLA Ops:
  0.7 2.8 %copy-start = (bf16[1,1,1,6,1024,512]{5,4,3,2,1,0:T(8,128)(2,1)S(1)}, bf16[1,1,1,6,1024,512]{5,4,3,2,1,0:T(8,128)(2,1)}, u32[]{:S(2)}) copy-start(bf16[1,1,1,6,1024,512]{5,4,3,2,1,0:T(8,128)(2,1)} %panel.1) | copy-start | bytes 18874372
  3.5 1.9 %copy-start.1 = (bf16[1,1,1,6,512,512]{5,4,3,2,1,0:T(8,128)(2,1)S(1)}, bf16[1,1,1,6,512,512]{5,4,3,2,1,0:T(8,128)(2,1)}, u32[]{:S(2)}) copy-start(bf16[1,1,1,6,512,512]{5,4,3,2,1,0:T(8,128)(2,1)} %face_block.1) | copy-start | bytes 9437188
  5.4 1.9 %copy-start.2 = (bf16[1,1,1,6,512,512]{5,4,3,2,1,0:T(8,128)(2,1)S(1)}, bf16[1,1,1,6,512,512]{5,4,3,2,1,0:T(8,128)(2,1)}, u32[]{:S(2)}) copy-start(bf16[1,1,1,6,512,512]{5,4,3,2,1,0:T(8,128)(2,1)} %deluxe_inv.1) | copy-start | bytes 9437188
  7.3 0.9 %copy-start.3 = (bf16[1,1,1,6,32,512]{5,4,3,2,1,0:T(8,128)(2,1)S(1)}, bf16[1,1,1,6,32,512]{5,4,3,2,1,0:T(8,128)(2,1)}, u32[]{:S(2)}) copy-start(bf16[1,1,1,6,32,512]{5,4,3,2,1,0:T(8,128)(2,1)} %residual.1) | copy-start | bytes 589828
  8.2 0.9 %copy-start.4 = (bf16[1,1,1,6,24,512]{5,4,3,2,1,0:T(8,128)(2,1)S(1)}, bf16[1,1,1,6,24,512]{5,4,3,2,1,0:T(8,128)(2,1)}, u32[]{:S(2)}) copy-start(bf16[1,1,1,6,24,512]{5,4,3,2,1,0:T(8,128)(2,1)} %basis.1) | copy-start | bytes 442372
  9.1 0.7 %copy-start.5 = (s32[1,1,1,6]{3,2,1,0:T(1,128)S(1)}, s32[1,1,1,6]{3,2,1,0:T(1,128)}, u32[]{:S(2)}) copy-start(s32[1,1,1,6]{3,2,1,0:T(1,128)} %size_ref.1) | copy-start | bytes 76
  9.7 0.7 %copy-start.6 = (f32[1,1,1,32]{3,2,1,0:T(1,128)S(1)}, f32[1,1,1,32]{3,2,1,0:T(1,128)}, u32[]{:S(2)}) copy-start(f32[1,1,1,32]{3,2,1,0:T(1,128)} %scale_ref.1) | copy-start | bytes 388

commit v2 on v1

--- a/solution.py
+++ b/solution.py
@@ -55,7 +55,7 @@
         )
 
     c_size = pltpu.make_async_copy(size_ref.at[0, 0], size_s, sem_small.at[0])
-    c_idx = pltpu.make_async_copy(idx_ref.at[0, 0, 0], idx_v, sem_small.at[1])
+    c_idx = pltpu.make_async_copy(idx_ref, idx_v, sem_small.at[1])
     c_scale = pltpu.make_async_copy(scale_ref.at[0, 0], scale_v, sem_small.at[2])
     c_res = pltpu.make_async_copy(residual.at[0, 0, 0], res_v, sem_res)
     c_bas = pltpu.make_async_copy(basis.at[0, 0, 0], bas_v, sem_bas)
@@ -80,7 +80,7 @@
     row = lax.broadcasted_iota(jnp.int32, (256, 1), 0)
     unknown = (row & 31) + 32 * (row >> 7)
     for s in ORDER:
-        onehot = jnp.where(unknown == idx_v[pl.ds(s, 1), :], 1.0, 0.0).astype(BF16)
+        onehot = jnp.where(unknown == idx_v[s], 1.0, 0.0).astype(BF16)
         expanded[s] = dot_nn(onehot, bas_v[s]).astype(BF16)
 
     c_res.wait()
@@ -153,6 +153,8 @@
     entries = basis.shape[4]
     owned = coarse_scale.shape[-1]
     dma = pltpu.SemaphoreType.DMA
+    operands = (residual, panel, face_block, deluxe_inv, basis, face_size, coarse_idx.reshape((slots, 1, entries)), coarse_scale)
+    operands = [pltpu.with_memory_space_constraint(operand, pltpu.HBM) for operand in operands]
     return pl.pallas_call(
         functools.partial(kernel, sizes),
         out_shape=jax.ShapeDtypeStruct(residual.shape, BF16),
@@ -165,7 +167,7 @@
             pltpu.VMEM((slots, width, width), BF16),
             pltpu.VMEM((slots, entries, width), BF16),
             pltpu.SMEM((1, slots), jnp.int32),
-            pltpu.VMEM((slots, entries), jnp.int32),
+            pltpu.VMEM((slots, 1, entries), jnp.int32),
             pltpu.VMEM((1, owned), F32),
             pltpu.VMEM((slots, 8 * owned, width), BF16),
             pltpu.VMEM((slots, rows, width), F32),
@@ -179,9 +181,9 @@
             dma((6,)), dma((6,)), dma((6,)), dma((6,)), dma((6,)), dma((6,)),
         ],
         compiler_params=pltpu.CompilerParams(
-            collective_id=0, has_side_effects=True, vmem_limit_bytes=40 * 1024 * 1024
+            collective_id=0, has_side_effects=True, vmem_limit_bytes=32 * 1024 * 1024
         ),
-    )(residual, panel, face_block, deluxe_inv, basis, face_size, coarse_idx, coarse_scale)
+    )(*operands)
 
 
 def solution(mesh):

time: 32.5 us -> 24.9 us (0.77)
  local copies, waits for them, and re-layouts: 11.1 us -> 0.68 us
  Pallas kernels: 21.1 us -> 24.1 us
    unnamed x16 -> x1, local copies, waits for them, and re-layouts: 11.1 us -> 0.68 us
    pallas_call x1, Pallas kernels: 21.1 us -> 24.1 us  [on_device(): pl.pallas_call(functools.partial(kernel, sizes), out_shape=jax.ShapeDtype...]
where the time goes in v2:
time: 24.9 us; the launch traced here: 24.8 us
  Pallas kernels  24.1 us (97%)
  local copies, waits for them, and re-layouts  0.68 us (3%)
    pallas_call x1, Pallas kernels, on_device(): pl.pallas_call(functools.partial(kernel, sizes), out_shape=jax.ShapeDtype...  24.1 us
    unnamed x1, local copies, waits for them, and re-layouts  0.68 us

profile of v2, /device:TPU:0, one launch (start us, length us, event | category | flops | bytes accessed | tf_op | source)
XLA Modules:
  0.0 24.8 jit_solution(8049433333024855878)
XLA Ops:
  0.0 24.1 %shard_map.82 = bf16[1,1,1,6,32,512]{5,4,3,2,1,0:T(8,128)(2,1)S(1)} custom-call(bf16[1,1,1,6,32,512]{5,4,3,2,1,0:T(8,128)(2,1)} %residual.1, bf16[1,1,1,6,1024,512]{5,4,3,2,1,0:T(8,128)(2,1)} %panel.1, bf16[1,1,1,6,512,512]{5,4,3,2,1,0:T(8,128)(2,1)} %face_block.1, bf16[1,1,1,6,512,512]{5,4,3,2,1,0:T(8,128)(2,1)} %deluxe_inv.1, ...), custom_call_target="tpu_custom_call" | custom-call | tf_op jit(solution)/shard_map/pallas_call | solution.py:158
  24.1 0.7 %copy.10 = bf16[1,1,1,6,32,512]{5,4,3,2,1,0:T(8,128)(2,1)} copy(bf16[1,1,1,6,32,512]{5,4,3,2,1,0:T(8,128)(2,1)S(1)} %shard_map.82) | data formatting | bytes 393216

commit v3 on v2

--- a/solution.py
+++ b/solution.py
@@ -22,14 +22,40 @@
     return lax.dot_general(a, b, (((1,), (0,)), ((), ())), preferred_element_type=F32)
 
 
+def plan(sizes):
+    def wrap(offset):
+        return tuple(c % n for c, n in zip(offset, sizes))
+
+    def plus(a, b):
+        return wrap(tuple(x + y for x, y in zip(a, b)))
+
+    units = []
+    for slot in range(6):
+        step = [0, 0, 0]
+        step[slot // 2] = 1 if slot % 2 == 0 else -1
+        units.append(wrap(step))
+    near = list(dict.fromkeys(units))
+    targets = {}
+    for u in near:
+        for d in [u] + [plus(u, t) for t in near]:
+            if any(d):
+                targets.setdefault(d, []).append(u)
+    starts, total = {}, 0
+    for d in targets:
+        starts[d] = total
+        total += 8 * (len(targets[d]) + (2 if d in near else 0))
+    minus = lambda a, b: wrap(tuple(x - y for x, y in zip(a, b)))
+    return units, near, targets, starts, total, minus
+
+
 def kernel(
     sizes,
     residual, panel, face_block, deluxe_inv, basis, size_ref, idx_ref, scale_ref,
     out_ref,
     res_v, pan_v, fb_v, inv_v, bas_v, size_s, idx_v, scale_v,
-    expanded, applied, recv1, averaged, send2, recv2, send3, recv3,
+    expanded, applied, recv1, averaged, send2, recv2,
     sem_res, sem_pan, sem_fb, sem_inv, sem_bas, sem_small,
-    ssem1, rsem1, ssem2, rsem2, ssem3, rsem3,
+    ssem1, rsem1, ssem2, rsem2,
 ):
     me = [lax.axis_index(name) for name in AXES]
 
@@ -40,13 +66,18 @@
         coords[axis] = lax.rem(me[axis] + step, sizes[axis])
         return tuple(coords)
 
+    units, near, targets, starts, _, minus = plan(sizes)
+
+    def at_offset(offset):
+        return tuple(lax.rem(m + c, n) for m, c, n in zip(me, offset, sizes))
+
     barrier = pltpu.get_barrier_semaphore()
-    for slot in range(6):
-        pl.semaphore_signal(barrier, inc=1, device_id=neighbour(slot), device_id_type=MESH)
+    for d in targets:
+        pl.semaphore_signal(barrier, inc=1, device_id=at_offset(d), device_id_type=MESH)
 
     def remote(src, dst, ssem, rsem, slot):
         return pltpu.make_async_remote_copy(
-            src_ref=src.at[slot] if src.shape[0] == 6 else src.at[0],
+            src_ref=src.at[slot],
             dst_ref=dst.at[slot ^ 1],
             send_sem=ssem.at[slot],
             recv_sem=rsem.at[slot ^ 1],
@@ -93,7 +124,7 @@
         value = dot_nt(masked, fb_v[s]) - through
         applied[s] = jnp.where(live[s], value, 0.0)
         if k == 0:
-            pl.semaphore_wait(barrier, 6)
+            pl.semaphore_wait(barrier, len(targets))
         remote(applied, recv1, ssem1, rsem1, s).start()
 
     group8 = lax.broadcasted_iota(jnp.int32, (8, 128), 1) >> 5
@@ -107,7 +138,22 @@
     def spread(tile):
         return jnp.concatenate([jnp.where(group8 == j, tile, 0.0) for j in range(4)], axis=0)
 
+    messages = []
+    for i, d in enumerate(targets):
+        rows = pl.ds(starts[d], 8 * (len(targets[d]) + (2 if d in near else 0)))
+        messages.append(pltpu.make_async_remote_copy(
+            src_ref=send2.at[rows],
+            dst_ref=recv2.at[rows],
+            send_sem=ssem2.at[i],
+            recv_sem=rsem2.at[i],
+            device_id=at_offset(d),
+            device_id_type=MESH,
+        ))
+
+    c_scale.wait()
+    scale = jnp.broadcast_to(jnp.concatenate([scale_v[...]] * 4, axis=1), (8, 128))
     own = jnp.zeros((8, 128), F32)
+    outward = {}
     for s in ORDER:
         remote(applied, recv1, ssem1, rsem1, s ^ 1).wait_recv()
         c_inv[s].wait()
@@ -116,35 +162,50 @@
         averaged[s] = value
         split = dot_nt(value, expanded[s])
         own = own + packed(split[:, 0:128])
-        send2[s] = packed(split[:, 128:256])
-        remote(send2, recv2, ssem2, rsem2, s).start()
-
-    c_scale.wait()
-    scale = jnp.concatenate([scale_v[...]] * 4, axis=1)
-    for s in ORDER:
-        remote(send2, recv2, ssem2, rsem2, s ^ 1).wait_recv()
-        own = own + recv2[s]
-    correction = own * scale
-    send3[0] = correction
-    for s in ORDER:
-        remote(send3, recv3, ssem3, rsem3, s).start()
+        part = packed(split[:, 128:256])
+        outward[units[s]] = outward[units[s]] + part if units[s] in outward else part
+    for i, d in enumerate(targets):
+        at = starts[d]
+        for u in targets[d]:
+            send2[pl.ds(at, 8)] = outward[u]
+            at += 8
+        if d in near:
+            send2[pl.ds(at, 8)] = own
+            send2[pl.ds(at + 8, 8)] = scale
+        messages[i].start()
+
+    zero = (0, 0, 0)
+    coarse = dict(outward)
+    coarse[zero] = own
+    scales = {zero: scale}
+    for i, d in enumerate(targets):
+        messages[i].wait_recv()
+        at = starts[d]
+        for u in targets[d]:
+            key = minus(u, d)
+            coarse[key] = coarse[key] + recv2[pl.ds(at, 8)]
+            at += 8
+        if d in near:
+            key = minus(zero, d)
+            coarse[key] = coarse[key] + recv2[pl.ds(at, 8)]
+            scales[key] = recv2[pl.ds(at + 8, 8)]
+    correction = {key: coarse[key] * scales[key] for key in coarse}
 
     def halves(tile):
         high = tile.astype(BF16)
         return high, (tile - high.astype(F32)).astype(BF16)
 
-    mine = spread(correction)
-    for s in ORDER:
-        remote(send3, recv3, ssem3, rsem3, s ^ 1).wait_recv()
-        table = jnp.concatenate([mine, spread(recv3[s])], axis=1)
+    mine = spread(correction[zero])
+    for s in ORDER:
+        table = jnp.concatenate([mine, spread(correction[units[s]])], axis=1)
         high, low = halves(table)
         added = dot_nn(high, expanded[s]) + dot_nn(low, expanded[s])
         out_ref[0, 0, 0, s] = jnp.where(live[s], averaged[s].astype(F32) + added, 0.0).astype(BF16)
 
     for s in ORDER:
         remote(applied, recv1, ssem1, rsem1, s).wait_send()
-        remote(send2, recv2, ssem2, rsem2, s).wait_send()
-        remote(send3, recv3, ssem3, rsem3, s).wait_send()
+    for message in messages:
+        message.wait_send()
 
 
 def on_device(sizes, residual, panel, face_block, deluxe_inv, basis, face_size, coarse_idx, coarse_scale):
@@ -153,6 +214,8 @@
     entries = basis.shape[4]
     owned = coarse_scale.shape[-1]
     dma = pltpu.SemaphoreType.DMA
+    _, _, targets, _, total, _ = plan(sizes)
+    count = len(targets)
     operands = (residual, panel, face_block, deluxe_inv, basis, face_size, coarse_idx.reshape((slots, 1, entries)), coarse_scale)
     operands = [pltpu.with_memory_space_constraint(operand, pltpu.HBM) for operand in operands]
     return pl.pallas_call(
@@ -173,12 +236,10 @@
             pltpu.VMEM((slots, rows, width), F32),
             pltpu.VMEM((slots, rows, width), F32),
             pltpu.VMEM((slots, rows, width), BF16),
-            pltpu.VMEM((slots, 8, 128), F32),
-            pltpu.VMEM((slots, 8, 128), F32),
-            pltpu.VMEM((1, 8, 128), F32),
-            pltpu.VMEM((slots, 8, 128), F32),
+            pltpu.VMEM((total, 128), F32),
+            pltpu.VMEM((total, 128), F32),
             dma, dma((6,)), dma((6,)), dma((6,)), dma, dma((3,)),
-            dma((6,)), dma((6,)), dma((6,)), dma((6,)), dma((6,)), dma((6,)),
+            dma((6,)), dma((6,)), dma((count,)), dma((count,)),
         ],
         compiler_params=pltpu.CompilerParams(
             collective_id=0, has_side_effects=True, vmem_limit_bytes=32 * 1024 * 1024

time: 24.9 us -> 23.5 us (0.944)
  Pallas kernels: 24.1 us -> 22.7 us
    pallas_call x1, Pallas kernels: 24.1 us -> 22.7 us  [on_device(): pl.pallas_call(functools.partial(kernel, sizes), out_shape=jax.ShapeDtype...]
where the time goes in v3:
time: 23.5 us; the launch traced here: 23.3 us
  Pallas kernels  22.7 us (97%)
  local copies, waits for them, and re-layouts  0.68 us (3%)
    pallas_call x1, Pallas kernels, on_device(): pl.pallas_call(functools.partial(kernel, sizes), out_shape=jax.ShapeDtype...  22.7 us
    unnamed x1, local copies, waits for them, and re-layouts  0.68 us

profile of v3, /device:TPU:0, one launch (start us, length us, event | category | flops | bytes accessed | tf_op | source)
XLA Modules:
  0.0 23.3 jit_solution(3210203675547022089)
XLA Ops:
  0.0 22.7 %shard_map.82 = bf16[1,1,1,6,32,512]{5,4,3,2,1,0:T(8,128)(2,1)S(1)} custom-call(bf16[1,1,1,6,32,512]{5,4,3,2,1,0:T(8,128)(2,1)} %residual.1, bf16[1,1,1,6,1024,512]{5,4,3,2,1,0:T(8,128)(2,1)} %panel.1, bf16[1,1,1,6,512,512]{5,4,3,2,1,0:T(8,128)(2,1)} %face_block.1, bf16[1,1,1,6,512,512]{5,4,3,2,1,0:T(8,128)(2,1)} %deluxe_inv.1, ...), custom_call_target="tpu_custom_call" | custom-call | tf_op jit(solution)/shard_map/pallas_call | solution.py:221
  22.7 0.7 %copy.10 = bf16[1,1,1,6,32,512]{5,4,3,2,1,0:T(8,128)(2,1)} copy(bf16[1,1,1,6,32,512]{5,4,3,2,1,0:T(8,128)(2,1)S(1)} %shard_map.82) | data formatting | bytes 393216

commit v4 on v3

--- a/solution.py
+++ b/solution.py
@@ -106,14 +106,6 @@
     c_size.wait()
     live = [lane < size_s[0, s] for s in range(6)]
 
-    c_idx.wait()
-    c_bas.wait()
-    row = lax.broadcasted_iota(jnp.int32, (256, 1), 0)
-    unknown = (row & 31) + 32 * (row >> 7)
-    for s in ORDER:
-        onehot = jnp.where(unknown == idx_v[s], 1.0, 0.0).astype(BF16)
-        expanded[s] = dot_nn(onehot, bas_v[s]).astype(BF16)
-
     c_res.wait()
     for k, s in enumerate(ORDER):
         c_pan[s].wait()
@@ -126,6 +118,14 @@
         if k == 0:
             pl.semaphore_wait(barrier, len(targets))
         remote(applied, recv1, ssem1, rsem1, s).start()
+
+    c_idx.wait()
+    c_bas.wait()
+    row = lax.broadcasted_iota(jnp.int32, (256, 1), 0)
+    unknown = (row & 31) + 32 * (row >> 7)
+    for s in ORDER:
+        onehot = jnp.where(unknown == idx_v[s], 1.0, 0.0).astype(BF16)
+        expanded[s] = dot_nn(onehot, bas_v[s]).astype(BF16)
 
     group8 = lax.broadcasted_iota(jnp.int32, (8, 128), 1) >> 5
 

time: 23.5 us -> 22.9 us (0.974)
  Pallas kernels: 22.7 us -> 22.1 us
    pallas_call x1, Pallas kernels: 22.7 us -> 22.1 us  [on_device(): pl.pallas_call(functools.partial(kernel, sizes), out_shape=jax.ShapeDtype...]
where the time goes in v4:
time: 22.9 us; the launch traced here: 22.8 us
  Pallas kernels  22.1 us (97%)
  local copies, waits for them, and re-layouts  0.68 us (3%)
    pallas_call x1, Pallas kernels, on_device(): pl.pallas_call(functools.partial(kernel, sizes), out_shape=jax.ShapeDtype...  22.1 us
    unnamed x1, local copies, waits for them, and re-layouts  0.68 us

profile of v4, /device:TPU:0, one launch (start us, length us, event | category | flops | bytes accessed | tf_op | source)
XLA Modules:
  0.0 22.8 jit_solution(5917319808048687813)
XLA Ops:
  0.0 22.1 %shard_map.82 = bf16[1,1,1,6,32,512]{5,4,3,2,1,0:T(8,128)(2,1)S(1)} custom-call(bf16[1,1,1,6,32,512]{5,4,3,2,1,0:T(8,128)(2,1)} %residual.1, bf16[1,1,1,6,1024,512]{5,4,3,2,1,0:T(8,128)(2,1)} %panel.1, bf16[1,1,1,6,512,512]{5,4,3,2,1,0:T(8,128)(2,1)} %face_block.1, bf16[1,1,1,6,512,512]{5,4,3,2,1,0:T(8,128)(2,1)} %deluxe_inv.1, ...), custom_call_target="tpu_custom_call" | custom-call | tf_op jit(solution)/shard_map/pallas_call | solution.py:221
  22.1 0.7 %copy.10 = bf16[1,1,1,6,32,512]{5,4,3,2,1,0:T(8,128)(2,1)} copy(bf16[1,1,1,6,32,512]{5,4,3,2,1,0:T(8,128)(2,1)S(1)} %shard_map.82) | data formatting | bytes 393216

commit v5 on v4

--- a/solution.py
+++ b/solution.py
@@ -154,6 +154,19 @@
     scale = jnp.broadcast_to(jnp.concatenate([scale_v[...]] * 4, axis=1), (8, 128))
     own = jnp.zeros((8, 128), F32)
     outward = {}
+    done, sent = [], []
+
+    def send(i, d):
+        at = starts[d]
+        for u in targets[d]:
+            send2[pl.ds(at, 8)] = outward[u]
+            at += 8
+        if d in near:
+            send2[pl.ds(at, 8)] = own
+            send2[pl.ds(at + 8, 8)] = scale
+        messages[i].start()
+        sent.append(d)
+
     for s in ORDER:
         remote(applied, recv1, ssem1, rsem1, s ^ 1).wait_recv()
         c_inv[s].wait()
@@ -164,15 +177,14 @@
         own = own + packed(split[:, 0:128])
         part = packed(split[:, 128:256])
         outward[units[s]] = outward[units[s]] + part if units[s] in outward else part
+        done.append(s)
+        for i, d in enumerate(targets):
+            ready = all(t in done for t in range(6) if units[t] in targets[d])
+            if d not in sent and d not in near and ready:
+                send(i, d)
     for i, d in enumerate(targets):
-        at = starts[d]
-        for u in targets[d]:
-            send2[pl.ds(at, 8)] = outward[u]
-            at += 8
-        if d in near:
-            send2[pl.ds(at, 8)] = own
-            send2[pl.ds(at + 8, 8)] = scale
-        messages[i].start()
+        if d not in sent:
+            send(i, d)
 
     zero = (0, 0, 0)
     coarse = dict(outward)
@@ -199,7 +211,9 @@
     for s in ORDER:
         table = jnp.concatenate([mine, spread(correction[units[s]])], axis=1)
         high, low = halves(table)
-        added = dot_nn(high, expanded[s]) + dot_nn(low, expanded[s])
+        both = dot_nn(jnp.concatenate([high, low], axis=0), expanded[s])
+        rows = high.shape[0]
+        added = both[0:rows] + both[rows:2 * rows]
         out_ref[0, 0, 0, s] = jnp.where(live[s], averaged[s].astype(F32) + added, 0.0).astype(BF16)
 
     for s in ORDER:

time: 22.9 us -> 21.9 us (0.956)
  Pallas kernels: 22.1 us -> 21.1 us
    pallas_call x1, Pallas kernels: 22.1 us -> 21.1 us  [on_device(): pl.pallas_call(functools.partial(kernel, sizes), out_shape=jax.ShapeDtype...]
where the time goes in v5:
time: 21.9 us; the launch traced here: 21.8 us
  Pallas kernels  21.1 us (96%)
  local copies, waits for them, and re-layouts  0.68 us (3%)
    pallas_call x1, Pallas kernels, on_device(): pl.pallas_call(functools.partial(kernel, sizes), out_shape=jax.ShapeDtype...  21.1 us
    unnamed x1, local copies, waits for them, and re-layouts  0.68 us

profile of v5, /device:TPU:0, one launch (start us, length us, event | category | flops | bytes accessed | tf_op | source)
XLA Modules:
  0.0 21.8 jit_solution(9503790817796148269)
XLA Ops:
  0.0 21.1 %shard_map.82 = bf16[1,1,1,6,32,512]{5,4,3,2,1,0:T(8,128)(2,1)S(1)} custom-call(bf16[1,1,1,6,32,512]{5,4,3,2,1,0:T(8,128)(2,1)} %residual.1, bf16[1,1,1,6,1024,512]{5,4,3,2,1,0:T(8,128)(2,1)} %panel.1, bf16[1,1,1,6,512,512]{5,4,3,2,1,0:T(8,128)(2,1)} %face_block.1, bf16[1,1,1,6,512,512]{5,4,3,2,1,0:T(8,128)(2,1)} %deluxe_inv.1, ...), custom_call_target="tpu_custom_call" | custom-call | tf_op jit(solution)/shard_map/pallas_call | solution.py:235
  21.1 0.7 %copy.10 = bf16[1,1,1,6,32,512]{5,4,3,2,1,0:T(8,128)(2,1)} copy(bf16[1,1,1,6,32,512]{5,4,3,2,1,0:T(8,128)(2,1)S(1)} %shard_map.82) | data formatting | bytes 393216
